TPU v7x, 128 devices: a whole 4x4x4 slice. The times are simulated.
128 devices in a mesh: dp: 4 (over x), row: 4 (over y_lo, core), col: 8 (over y_hi, z).
Axes of the slice: x: 4, y: 4 (y_hi: 2, y_lo: 2; y = y_hi * 2 + y_lo), z: 4, core: 2. Of those that a mesh axis runs over, the one named last changes fastest.
Arguments:
- tokens: bfloat16 [16400, 1024], P(('dp', 'row'), 'col'), may hold values from -6 to 6
- cotangent: float32 [16400, 1024], P(('dp', 'row'), 'col'), may hold values from -6 to 6
- attend_weight: bfloat16 [2, 1024, 3, 1024], P(None, 'row', None, 'col'), may hold values from -0.1875 to 0.1875
- output_weight: bfloat16 [2, 1024, 1024], P(None, 'col', 'row'), may hold values from -1.5 to 1.5
- up_weight: bfloat16 [2, 1024, 4096], P(None, 'row', 'col'), may hold values from -0.1875 to 0.1875
- down_weight: bfloat16 [2, 4096, 1024], P(None, 'col', 'row'), may hold values from -0.09375 to 0.09375
- norm_gain: float32 [2, 2, 1024], P(None, None, 'col'), may hold values from 0.1 to 1.9
- norm_shift: float32 [2, 2, 1024], P(None, None, 'col'), may hold values from -2 to 2
- attend_bias: float32 [2, 2, 1024], P(None, None, 'col'), may hold values from -3 to 3
- branch_bias: float32 [2, 2, 1024], P(None, None, 'col'), may hold values from -2 to 2
- layer_scale: float32 [2, 2, 1024], P(None, None, 'col'), may hold values from 0.3 to 1.5
- hidden_bias: float32 [2, 4096], P(None, 'col'), may hold values from -3 to 3
Outputs:
- block_output: float32 [16400, 1024], P(('dp', 'row'), 'col')
- tokens_grad: float32 [16400, 1024], P(('dp', 'row'), 'col')
- attend_grad: float32 [2, 1024, 3, 1024], P(None, 'row', None, 'col')
- output_grad: float32 [2, 1024, 1024], P(None, 'col', 'row')
- up_grad: float32 [2, 1024, 4096], P(None, 'row', 'col')
- down_grad: float32 [2, 4096, 1024], P(None, 'col', 'row')
- gain_grad: float32 [2, 2, 1024], P(None, None, 'col')
- shift_grad: float32 [2, 2, 1024], P(None, None, 'col')
- bias_grad: float32 [2, 2, 1024], P(None, None, 'col')
- branch_grad: float32 [2, 2, 1024], P(None, None, 'col')
- scale_grad: float32 [2, 2, 1024], P(None, None, 'col')
- hidden_grad: float32 [2, 4096], P(None, 'col')
All inputs are finite; a program needn't handle non-finite values.
Results may differ from a plain program's by a relative error of at most 0.035.
Values may be sent and summed in bfloat16 or wider, within the bound.
A program may use at most 192 MiB of HBM per device.

v0:
```python
import jax
import jax.numpy as jnp
from jax import lax
from jax.sharding import PartitionSpec as P

MODEL_WIDTH = 1024
HEAD_DIM = 64
SEQ = 1025
LAYERS = 2
IMG_DEV = 1


EPS = 1e-06
ROOT_HALF = 0.7071067811865476
INV_ROOT_TWO_PI = 0.3989422804014327


def gelu_value(value):
    return 0.5 * value * (1.0 + lax.erf(value * ROOT_HALF))


def gelu_slope(value):
    return 0.5 * (1.0 + lax.erf(value * ROOT_HALF)) + value * INV_ROOT_TWO_PI * jnp.exp(
        -0.5 * value * value
    )


def contract_last(left, right):
    return lax.dot_general(
        left, right, (((1,), (1,)), ((), ())), preferred_element_type=jnp.float32
    )


def contract_first(left, right):
    return lax.dot_general(
        left, right, (((0,), (0,)), ((), ())), preferred_element_type=jnp.float32
    )


def normalize(residual_input, gain, shift):
    whole, gain_all, shift_all = (
        lax.all_gather(residual_input.astype(jnp.bfloat16), "col", axis=1, tiled=True).astype(
            residual_input.dtype
        ),
        lax.all_gather(gain.astype(jnp.bfloat16), "col", axis=0, tiled=True).astype(gain.dtype),
        lax.all_gather(shift.astype(jnp.bfloat16), "col", axis=0, tiled=True).astype(shift.dtype),
    )
    row_mean = jnp.mean(whole, axis=1, keepdims=True)
    meansq = jnp.mean(whole * whole, axis=1, keepdims=True)
    inverse_deviation = lax.rsqrt(meansq - row_mean * row_mean + EPS)
    normed = ((whole - row_mean) * inverse_deviation * gain_all + shift_all).astype(jnp.bfloat16)
    return (normed, row_mean, inverse_deviation)


def norm_backward(gradient_value, residual_input, row_mean, inverse_deviation, gain):
    centered_normed = (residual_input - row_mean) * inverse_deviation
    scaled_output = gradient_value * gain
    total_sum, along_dimension = lax.psum(
        (
            jnp.sum(scaled_output, axis=1, keepdims=True),
            jnp.sum(scaled_output * centered_normed, axis=1, keepdims=True),
        ),
        "col",
    )
    backward_pass = inverse_deviation * (
        scaled_output - total_sum / MODEL_WIDTH - centered_normed * (along_dimension / MODEL_WIDTH)
    )
    return (
        backward_pass,
        jnp.sum(gradient_value * centered_normed, axis=0),
        jnp.sum(gradient_value, axis=0),
    )


def gather_layer(attend_w, output_w, up_w, down_w):
    return (
        lax.all_gather(attend_w, "row", axis=0, tiled=True),
        lax.all_gather(output_w, "row", axis=1, tiled=True),
        lax.all_gather(up_w, "row", axis=0, tiled=True),
        lax.all_gather(down_w, "row", axis=1, tiled=True),
    )


def branch_total(partial_value):
    return lax.psum_scatter(
        partial_value.astype(jnp.bfloat16), "col", scatter_dimension=1, tiled=True
    ).astype(jnp.float32)


def spread_grad(grad_low):
    return lax.all_gather(grad_low, "col", axis=1, tiled=True)


def input_total(partial_value):
    return lax.psum_scatter(
        partial_value.astype(jnp.bfloat16), "col", scatter_dimension=1, tiled=True
    ).astype(jnp.float32)


def attend(packed):
    rows = packed.shape[0]
    heads_here = packed.shape[2] // HEAD_DIM
    scale = HEAD_DIM ** (-0.5)
    blocks = packed.reshape(IMG_DEV, SEQ, 3, heads_here, HEAD_DIM)

    def one_image(item):
        query, key, value = (item[:, 0], item[:, 1], item[:, 2])
        scores = jnp.einsum("qhd,khd->hqk", query, key, preferred_element_type=jnp.float32) * scale
        top = jnp.max(scores, axis=-1, keepdims=True)
        expd = jnp.exp(scores - top)
        total_sum = jnp.sum(expd, axis=-1, keepdims=True)
        probs = (expd / total_sum).astype(jnp.bfloat16)
        result = jnp.einsum("hqk,khd->qhd", probs, value, preferred_element_type=jnp.float32)
        return (result.astype(jnp.bfloat16), (top + jnp.log(total_sum))[..., 0])

    result, logsum = lax.map(one_image, blocks)
    return (result.reshape(rows, heads_here * HEAD_DIM), logsum)


def attend_backward(packed, upstream, logsum):
    rows = packed.shape[0]
    heads_here = packed.shape[2] // HEAD_DIM
    scale = HEAD_DIM ** (-0.5)
    blocks = packed.reshape(IMG_DEV, SEQ, 3, heads_here, HEAD_DIM)
    grads = upstream.reshape(IMG_DEV, SEQ, heads_here, HEAD_DIM)

    def one_image(item):
        tile, dout, lse_rows = item
        query, key, value = (tile[:, 0], tile[:, 1], tile[:, 2])
        scores = jnp.einsum("qhd,khd->hqk", query, key, preferred_element_type=jnp.float32) * scale
        probs = jnp.exp(scores - lse_rows[..., None])
        rounded = probs.astype(jnp.bfloat16)
        dprobs = jnp.einsum("qhd,khd->hqk", dout, value, preferred_element_type=jnp.float32)
        dscores = (probs * (dprobs - jnp.sum(probs * dprobs, axis=-1, keepdims=True))).astype(
            jnp.bfloat16
        )
        dquery = (
            jnp.einsum("hqk,khd->qhd", dscores, key, preferred_element_type=jnp.float32) * scale
        )
        dkey = (
            jnp.einsum("hqk,qhd->khd", dscores, query, preferred_element_type=jnp.float32) * scale
        )
        dvalue = jnp.einsum("hqk,qhd->khd", rounded, dout, preferred_element_type=jnp.float32)
        return jnp.stack([dquery, dkey, dvalue], axis=1).astype(jnp.bfloat16)

    result = lax.map(one_image, (blocks, grads, logsum))
    return result.reshape(rows, 3, heads_here * HEAD_DIM)


def forward_layer(residual_input, weights, params):
    attend_full, output_full, up_full, down_full = weights
    gains, shifts, abias, bbias, scales, hbias = params
    normed_one, mean_one, rstd_one = normalize(residual_input, gains[0], shifts[0])
    packed = jnp.einsum("nd,dkc->nkc", normed_one, attend_full, preferred_element_type=jnp.float32)
    bias = jnp.stack([abias[0], jnp.zeros_like(abias[0]), abias[1]])
    packed = (packed + bias).astype(jnp.bfloat16)
    att, logsum = attend(packed)
    branch_one = (
        branch_total(jnp.dot(att, output_full, preferred_element_type=jnp.float32)) + bbias[0]
    )
    middle = residual_input + scales[0] * branch_one
    normed_two, mean_two, rstd_two = normalize(middle, gains[1], shifts[1])
    hidden = jnp.dot(normed_two, up_full, preferred_element_type=jnp.float32) + hbias
    active = gelu_value(hidden).astype(jnp.bfloat16)
    branch_two = (
        branch_total(jnp.dot(active, down_full, preferred_element_type=jnp.float32)) + bbias[1]
    )
    result = middle + scales[1] * branch_two
    saved = (
        residual_input,
        normed_one,
        mean_one,
        rstd_one,
        packed,
        att,
        logsum,
        branch_one,
        middle,
        normed_two,
        mean_two,
        rstd_two,
        hidden,
        active,
        branch_two,
    )
    return (result, saved)


def backward_layer(gradient_value, saved, weights, params):
    (
        residual_input,
        normed_one,
        mean_one,
        rstd_one,
        packed,
        att,
        logsum,
        branch_one,
        middle,
        normed_two,
        mean_two,
        rstd_two,
        hidden,
        active,
        branch_two,
    ) = saved
    attend_full, output_full, up_full, down_full = weights
    gains, shifts, abias, bbias, scales, hbias = params
    scale_two = jnp.sum(gradient_value * branch_two, axis=0)
    dbranch_two = (gradient_value * scales[1]).astype(jnp.bfloat16)
    bias_two = jnp.sum(dbranch_two.astype(jnp.float32), axis=0)
    dfull_two = spread_grad(dbranch_two)
    dactive = contract_last(dfull_two, down_full)
    dhidden = (dactive * gelu_slope(hidden)).astype(jnp.bfloat16)
    hidden_sum = jnp.sum(dhidden.astype(jnp.float32), axis=0)
    down_part = contract_first(active, dfull_two)
    up_part = contract_first(normed_two, dhidden)
    dnormed_two = input_total(contract_last(dhidden, up_full))
    dmiddle, gain_two, shift_two = norm_backward(dnormed_two, middle, mean_two, rstd_two, gains[1])
    dmiddle = dmiddle + gradient_value
    scale_one = jnp.sum(dmiddle * branch_one, axis=0)
    dbranch_one = (dmiddle * scales[0]).astype(jnp.bfloat16)
    bias_one = jnp.sum(dbranch_one.astype(jnp.float32), axis=0)
    dfull_one = spread_grad(dbranch_one)
    datt = contract_last(dfull_one, output_full).astype(jnp.bfloat16)
    output_part = contract_first(att, dfull_one)
    dpacked = attend_backward(packed, datt, logsum)
    dpacked_wide = dpacked.astype(jnp.float32)
    attend_sums = jnp.stack(
        [jnp.sum(dpacked_wide[:, 0], axis=0), jnp.sum(dpacked_wide[:, 2], axis=0)]
    )
    attend_part = jnp.einsum("nd,nkc->dkc", normed_one, dpacked, preferred_element_type=jnp.float32)
    dnormed_one = input_total(
        jnp.einsum("nkc,dkc->nd", dpacked, attend_full, preferred_element_type=jnp.float32)
    )
    dresid, gain_one, shift_one = norm_backward(
        dnormed_one, residual_input, mean_one, rstd_one, gains[0]
    )
    dresid = dresid + dmiddle
    summed = (
        lax.psum_scatter(
            attend_part.astype(jnp.bfloat16), "row", scatter_dimension=0, tiled=True
        ).astype(jnp.float32),
        lax.psum_scatter(
            output_part.astype(jnp.bfloat16), "row", scatter_dimension=1, tiled=True
        ).astype(jnp.float32),
        lax.psum_scatter(
            up_part.astype(jnp.bfloat16), "row", scatter_dimension=0, tiled=True
        ).astype(jnp.float32),
        lax.psum_scatter(
            down_part.astype(jnp.bfloat16), "row", scatter_dimension=1, tiled=True
        ).astype(jnp.float32),
    )
    summed = (
        lax.psum(summed[0].astype(jnp.bfloat16), "dp").astype(jnp.float32),
        lax.psum(summed[1].astype(jnp.bfloat16), "dp").astype(jnp.float32),
        lax.psum(summed[2].astype(jnp.bfloat16), "dp").astype(jnp.float32),
        lax.psum(summed[3].astype(jnp.bfloat16), "dp").astype(jnp.float32),
    )
    small = lax.psum(
        (
            jnp.stack([gain_one, gain_two]),
            jnp.stack([shift_one, shift_two]),
            attend_sums,
            jnp.stack([bias_one, bias_two]),
            jnp.stack([scale_one, scale_two]),
            hidden_sum,
        ),
        ("dp", "row"),
    )
    return (dresid, tuple(summed) + tuple(small))


def on_device(
    tokens,
    cotangent,
    attend_weight,
    output_weight,
    up_weight,
    down_weight,
    norm_gain,
    norm_shift,
    attend_bias,
    branch_bias,
    layer_scale,
    hidden_bias,
):
    residual_input = tokens.astype(jnp.float32)
    saved_all = []
    gathered = []
    params_all = []
    for layer in range(LAYERS):
        weights = gather_layer(
            attend_weight[layer], output_weight[layer], up_weight[layer], down_weight[layer]
        )
        params = (
            norm_gain[layer],
            norm_shift[layer],
            attend_bias[layer],
            branch_bias[layer],
            layer_scale[layer],
            hidden_bias[layer],
        )
        residual_input, saved = forward_layer(residual_input, weights, params)
        saved_all.append(saved)
        gathered.append(weights)
        params_all.append(params)
    gradient_value = cotangent
    layer_grads = [0] * LAYERS
    for layer in reversed(range(LAYERS)):
        weights = gathered[layer]
        gradient_value, grads = backward_layer(
            gradient_value, saved_all[layer], weights, params_all[layer]
        )
        layer_grads[layer] = grads
    stacked = tuple(
        (jnp.stack([layer_grads[layer][index] for layer in range(LAYERS)]) for index in range(10))
    )
    return (residual_input, gradient_value) + stacked


def solution(mesh):
    placed = (
        P(("dp", "row"), "col"),
        P(("dp", "row"), "col"),
        P(None, "row", None, "col"),
        P(None, "col", "row"),
        P(None, "row", "col"),
        P(None, "col", "row"),
        P(None, None, "col"),
        P(None, None, "col"),
        P(None, None, "col"),
        P(None, None, "col"),
        P(None, None, "col"),
        P(None, "col"),
    )
    return jax.shard_map(
        on_device,
        mesh=mesh,
        in_specs=placed,
        out_specs=(
            P(("dp", "row"), "col"),
            P(("dp", "row"), "col"),
            P(None, "row", None, "col"),
            P(None, "col", "row"),
            P(None, "row", "col"),
            P(None, "col", "row"),
            P(None, None, "col"),
            P(None, None, "col"),
            P(None, None, "col"),
            P(None, None, "col"),
            P(None, None, "col"),
            P(None, "col"),
        ),
        check_vma=False,
    )
```

profile of v0, /device:TPU:0, one launch (start us, length us, event | category | flops | bytes accessed | tf_op | source)
XLA Modules:
  0.0 1681.9 jit_solution(1155542807535669310)
XLA Ops:
  10.0 24.7 %all-gather.12 = bf16[8,1,128]{2,1,0:T(2,128)(2,1)S(1)} all-gather(bf16[1,1,128]{2,1,0:T(2,128)(2,1)S(1)} %get-tuple-element.175), channel_id=1, replica_groups=mesh['dp'=4,'row'=4,'col'=8] {'col'}, dimensions={0}, use_global_device_ids=true | all-gather | bytes 2304 | tf_op jit(solution)/shard_map/all_gather | solution.py:45
  91.2 74.2 %reduce-scatter.49.cloned.1.call-done = bf16[128,1025]{1,0:T(8,128)(2,1)} async-done(((bf16[1024,1025]{1,0:T(8,128)(2,1)}), bf16[128,1025]{1,0:T(8,128)(2,1)}) %reduce-scatter.49.cloned.1.call-update) | async-done | bytes 262416
  271.1 78.8 %reduce-scatter.51.cloned.1.call-done = bf16[128,1025]{1,0:T(8,128)(2,1)} async-done(((bf16[1024,1025]{1,0:T(8,128)(2,1)}), bf16[128,1025]{1,0:T(8,128)(2,1)}) %reduce-scatter.51.cloned.1.call-update) | async-done | bytes 262416
  423.8 76.7 %reduce-scatter.53.cloned.1.call-done = bf16[128,1025]{1,0:T(8,128)(2,1)} async-done(((bf16[1024,1025]{1,0:T(8,128)(2,1)}), bf16[128,1025]{1,0:T(8,128)(2,1)}) %reduce-scatter.53.cloned.1.call-update) | async-done | bytes 262416
  608.3 78.8 %reduce-scatter.55.cloned.1.call-done = bf16[128,1025]{1,0:T(8,128)(2,1)} async-done(((bf16[1024,1025]{1,0:T(8,128)(2,1)}), bf16[128,1025]{1,0:T(8,128)(2,1)}) %reduce-scatter.55.cloned.1.call-update) | async-done | bytes 262416
  689.7 53.7 %all-gather.37.cloned.1.call-done = bf16[1025,1024]{1,0:T(8,128)(2,1)} async-done(((bf16[1025,128]{1,0:T(8,128)(2,1)}), bf16[1025,1024]{1,0:T(8,128)(2,1)}) %all-gather.37.cloned.1.call-update) | async-done | bytes 2099216 | tf_op jit(solution)/shard_map/all_gather | solution.py:91
  757.4 73.5 %reduce-scatter.57.cloned.1.call-done = bf16[128,1025]{1,0:T(8,128)(2,1)} async-done(((bf16[1024,1025]{1,0:T(8,128)(2,1)}), bf16[128,1025]{1,0:T(8,128)(2,1)}) %reduce-scatter.57.cloned.1.call-update) | async-done | bytes 262416
  833.1 21.9 %all-reduce.4 = (f32[1025,1]{0,1:T(1,128)S(1)}, f32[1025,1]{0,1:T(1,128)S(1)}) all-reduce(f32[1025,1]{0,1:T(1,128)S(1)} %broadcast_in_dim.74, f32[1025,1]{0,1:T(1,128)S(1)} %broadcast_in_dim.47), channel_id=1, replica_groups=mesh['dp'=4,'row'=4,'col'=8] {'col'}, use_global_device_ids=true, to_apply=%region_20.21 | all-reduce | flops 2050 | bytes 16400 | tf_op jit(solution)/shard_map/psum | solution.py:58
  860.1 53.1 %all-gather.39.cloned.1.call-done = bf16[1025,1024]{1,0:T(8,128)(2,1)} async-done(((bf16[1025,128]{1,0:T(8,128)(2,1)}), bf16[1025,1024]{1,0:T(8,128)(2,1)}) %all-gather.39.cloned.1.call-update) | async-done | bytes 2099216 | tf_op jit(solution)/shard_map/all_gather | solution.py:91
  953.7 74.6 %reduce-scatter.59.cloned.1.call-done = bf16[128,1025]{1,0:T(8,128)(2,1)} async-done(((bf16[1024,1025]{1,0:T(8,128)(2,1)}), bf16[128,1025]{1,0:T(8,128)(2,1)}) %reduce-scatter.59.cloned.1.call-update) | async-done | bytes 262416
  1030.6 21.9 %all-reduce.3 = (f32[1025,1]{0,1:T(1,128)S(1)}, f32[1025,1]{0,1:T(1,128)S(1)}) all-reduce(f32[1025,1]{0,1:T(1,128)S(1)} %broadcast_in_dim.76, f32[1025,1]{0,1:T(1,128)S(1)} %broadcast_in_dim.75), channel_id=1, replica_groups=mesh['dp'=4,'row'=4,'col'=8] {'col'}, use_global_device_ids=true, to_apply=%region_26.27 | all-reduce | flops 2050 | bytes 16400 | tf_op jit(solution)/shard_map/psum | solution.py:58
  1055.5 53.4 %all-gather.41.cloned.1.call-done = bf16[1025,1024]{1,0:T(8,128)(2,1)} async-done(((bf16[1025,128]{1,0:T(8,128)(2,1)}), bf16[1025,1024]{1,0:T(8,128)(2,1)}) %all-gather.41.cloned.1.call-update) | async-done | bytes 2099216 | tf_op jit(solution)/shard_map/all_gather | solution.py:91
  1121.8 74.5 %reduce-scatter.61.cloned.1.call-done = bf16[128,1025]{1,0:T(8,128)(2,1)} async-done(((bf16[1024,1025]{1,0:T(8,128)(2,1)}), bf16[128,1025]{1,0:T(8,128)(2,1)}) %reduce-scatter.61.cloned.1.call-update) | async-done | bytes 262416
  1198.6 21.9 %all-reduce.2 = (f32[1025,1]{0,1:T(1,128)S(1)}, f32[1025,1]{0,1:T(1,128)S(1)}) all-reduce(f32[1025,1]{0,1:T(1,128)S(1)} %broadcast_in_dim.78, f32[1025,1]{0,1:T(1,128)S(1)} %broadcast_in_dim.77), channel_id=1, replica_groups=mesh['dp'=4,'row'=4,'col'=8] {'col'}, use_global_device_ids=true, to_apply=%region_31.32 | all-reduce | flops 2050 | bytes 16400 | tf_op jit(solution)/shard_map/psum | solution.py:58
  1248.9 28.2 %all-gather.43.cloned.1.call-done = bf16[1025,1024]{1,0:T(8,128)(2,1)} async-done(((bf16[1025,128]{1,0:T(8,128)(2,1)}), bf16[1025,1024]{1,0:T(8,128)(2,1)}) %all-gather.43.cloned.1.call-update) | async-done | bytes 2099216 | tf_op jit(solution)/shard_map/all_gather | solution.py:91
  1321.5 21.4 %reduce-scatter.39.cloned.1.call-done = bf16[128,256]{1,0:T(8,128)(2,1)} async-done(((bf16[128,1024]{1,0:T(8,128)(2,1)}), bf16[128,256]{1,0:T(8,128)(2,1)}) %reduce-scatter.39.cloned.1.call-update) | async-done | bytes 65552 | tf_op jit(solution)/shard_map/reduce_scatter | solution.py:244
  1342.9 23.3 %reduce-scatter.35.cloned.1.call-done = bf16[256,3,128]{2,0,1:T(8,128)(2,1)} async-done(((bf16[1024,3,128]{2,0,1:T(8,128)(2,1)}), bf16[256,3,128]{2,0,1:T(8,128)(2,1)}) %reduce-scatter.35.cloned.1.call-update) | async-done | bytes 196624 | tf_op jit(solution)/shard_map/reduce_scatter | solution.py:241
  1366.1 24.2 %reduce-scatter.41.cloned.1.call-done = bf16[256,512]{1,0:T(8,128)(2,1)} async-done(((bf16[1024,512]{1,0:T(8,128)(2,1)}), bf16[256,512]{1,0:T(8,128)(2,1)}) %reduce-scatter.41.cloned.1.call-update) | async-done | bytes 262160 | tf_op jit(solution)/shard_map/reduce_scatter | solution.py:247
  1390.4 23.6 %reduce-scatter.45.cloned.1.call-done = bf16[512,256]{1,0:T(8,128)(2,1)} async-done(((bf16[512,1024]{1,0:T(8,128)(2,1)}), bf16[512,256]{1,0:T(8,128)(2,1)}) %reduce-scatter.45.cloned.1.call-update) | async-done | bytes 262160 | tf_op jit(solution)/shard_map/reduce_scatter | solution.py:250
  1435.0 22.4 %reduce-scatter.33.cloned.1.call-done = bf16[256,3,128]{2,0,1:T(8,128)(2,1)} async-done(((bf16[1024,3,128]{2,0,1:T(8,128)(2,1)}), bf16[256,3,128]{2,0,1:T(8,128)(2,1)}) %reduce-scatter.33.cloned.1.call-update) | async-done | bytes 196624 | tf_op jit(solution)/shard_map/reduce_scatter | solution.py:241
  1464.3 48.5 %all-reduce.8.cloned.1.call-done = (bf16[1,256,3,128]{3,1,2,0:T(8,128)(2,1)}, bf16[1,256,3,128]{3,1,2,0:T(8,128)(2,1)}, bf16[1,128,256]{2,1,0:T(8,128)(2,1)}, bf...) async-done(((bf16[1,256,3,128]{3,1,2,0:T(8,128)(2,1)}, ...) | async-done | bytes 1572880 | tf_op jit(solution)/shard_map/psum | solution.py:255
  1519.6 73.6 %reduce-scatter.63.cloned.1.call-done = bf16[128,1025]{1,0:T(8,128)(2,1)} async-done(((bf16[1024,1025]{1,0:T(8,128)(2,1)}), bf16[128,1025]{1,0:T(8,128)(2,1)}) %reduce-scatter.63.cloned.1.call-update) | async-done | bytes 262416
  1595.1 21.9 %all-reduce.1 = (f32[1025,1]{0,1:T(1,128)S(1)}, f32[1025,1]{0,1:T(1,128)S(1)}) all-reduce(f32[1025,1]{0,1:T(1,128)S(1)} %broadcast_in_dim.80, f32[1025,1]{0,1:T(1,128)S(1)} %broadcast_in_dim.79), channel_id=1, replica_groups=mesh['dp'=4,'row'=4,'col'=8] {'col'}, use_global_device_ids=true, to_apply=%region_37.38 | all-reduce | flops 2050 | bytes 16400 | tf_op jit(solution)/shard_map/psum | solution.py:58
  1618.5 52.9 %all-reduce = (f32[1,2,128]{2,1,0:T(2,128)S(1)}, f32[1,2,128]{2,1,0:T(2,128)S(1)}, f32[1,2,128]{2,1,0:T(2,128)S(1)}, f32[1,2,128]{2,1,0:T(2,128)S(1)}, f32[1,2,1...) all-reduce(f32[1,2,128]{2,1,0:T(2,128)S(1)} %maximum_bitcast_fusion, ...), channel_id=1, replica_groups=mesh['dp'=4,'row'=4,'col'=8] {'dp','row'}, use_global_device_ids=true, to_apply=%region_59.60 | all-reduce | flops 3584 | bytes 28672 | tf_op jit(solution)/shard_map/psum | solution.py:260
  (456 shorter events, 544.1 us)
Async XLA Ops:
  7.9 157.5 %reduce-scatter.49.cloned.1.call-start = ((), (), s32[]{:S(2)}) async-start(), calls=%async_computation.36 | async-start | bytes 2654208
  90.0 131.7 %all-gather.31.cloned.1.call-start = ((), (), s32[]{:S(2)}) async-start(), calls=%async_computation.17 | async-start | bytes 2377728 | tf_op jit(solution)/shard_map/all_gather | solution.py:42
  168.3 97.3 %all-gather.47.cloned.1.call-start = ((), (), s32[]{:S(2)}) async-start(), calls=%async_computation.33 | async-start | bytes 1310720 | tf_op jit(solution)/shard_map/all_gather | solution.py:80
  169.2 180.6 %reduce-scatter.51.cloned.1.call-start = ((), (), s32[]{:S(2)}) async-start(), calls=%async_computation.37 | async-start | bytes 2654208
  271.0 136.5 %all-gather.33.cloned.1.call-start = ((), (), s32[]{:S(2)}) async-start(), calls=%async_computation.18 | async-start | bytes 2377728 | tf_op jit(solution)/shard_map/all_gather | solution.py:42
  352.0 148.6 %reduce-scatter.53.cloned.1.call-start = ((), (), s32[]{:S(2)}) async-start(), calls=%async_computation.38 | async-start | bytes 2654208
  423.8 133.0 %all-gather.35.cloned.1.call-start = ((), (), s32[]{:S(2)}) async-start(), calls=%async_computation.19 | async-start | bytes 2377728 | tf_op jit(solution)/shard_map/all_gather | solution.py:42
  503.1 97.2 %all-gather.51.cloned.1.call-start = ((), (), s32[]{:S(2)}) async-start(), calls=%async_computation.35 | async-start | bytes 1310720 | tf_op jit(solution)/shard_map/all_gather | solution.py:80
  503.9 183.2 %reduce-scatter.55.cloned.1.call-start = ((), (), s32[]{:S(2)}) async-start(), calls=%async_computation.39 | async-start | bytes 2654208
  608.3 135.1 %all-gather.37.cloned.1.call-start = ((), (), s32[]{:S(2)}) async-start(), calls=%async_computation.20 | async-start | bytes 2377728 | tf_op jit(solution)/shard_map/all_gather | solution.py:91
  689.6 141.2 %reduce-scatter.57.cloned.1.call-start = ((), (), s32[]{:S(2)}) async-start(), calls=%async_computation.40 | async-start | bytes 2654208
  756.2 156.9 %all-gather.39.cloned.1.call-start = ((), (), s32[]{:S(2)}) async-start(), calls=%async_computation.21 | async-start | bytes 2377728 | tf_op jit(solution)/shard_map/all_gather | solution.py:91
  859.6 168.7 %reduce-scatter.59.cloned.1.call-start = ((), (), s32[]{:S(2)}) async-start(), calls=%async_computation.41 | async-start | bytes 2654208
  953.6 155.2 %all-gather.41.cloned.1.call-start = ((), (), s32[]{:S(2)}) async-start(), calls=%async_computation.22 | async-start | bytes 2377728 | tf_op jit(solution)/shard_map/all_gather | solution.py:91
  1055.3 141.0 %reduce-scatter.61.cloned.1.call-start = ((), (), s32[]{:S(2)}) async-start(), calls=%async_computation.42 | async-start | bytes 2654208
  1121.7 155.3 %all-gather.43.cloned.1.call-start = ((), (), s32[]{:S(2)}) async-start(), calls=%async_computation.23 | async-start | bytes 2377728 | tf_op jit(solution)/shard_map/all_gather | solution.py:91
  1233.1 109.8 %reduce-scatter.39.cloned.1.call-start = ((), (), s32[]{:S(2)}) async-start(), calls=%async_computation.27 | async-start | bytes 327680 | tf_op jit(solution)/shard_map/reduce_scatter | solution.py:244
  1234.5 131.6 %reduce-scatter.35.cloned.1.call-start = ((), (), s32[]{:S(2)}) async-start(), calls=%async_computation.25 | async-start | bytes 983040 | tf_op jit(solution)/shard_map/reduce_scatter | solution.py:241
  1239.4 151.0 %reduce-scatter.41.cloned.1.call-start = ((), (), s32[]{:S(2)}) async-start(), calls=%async_computation.28 | async-start | bytes 1310720 | tf_op jit(solution)/shard_map/reduce_scatter | solution.py:247
  1244.1 169.9 %reduce-scatter.45.cloned.1.call-start = ((), (), s32[]{:S(2)}) async-start(), calls=%async_computation.30 | async-start | bytes 1310720 | tf_op jit(solution)/shard_map/reduce_scatter | solution.py:250
  1248.8 186.2 %reduce-scatter.37.cloned.1.call-start = ((), (), s32[]{:S(2)}) async-start(), calls=%async_computation.26 | async-start | bytes 327680 | tf_op jit(solution)/shard_map/reduce_scatter | solution.py:244
  1308.9 148.5 %reduce-scatter.33.cloned.1.call-start = ((), (), s32[]{:S(2)}) async-start(), calls=%async_computation.24 | async-start | bytes 983040 | tf_op jit(solution)/shard_map/reduce_scatter | solution.py:241
  1318.1 194.7 %all-reduce.8.cloned.1.call-start = ((), (), s32[]{:S(2)}) async-start(), calls=%async_computation.44 | async-start | bytes 3145728 | tf_op jit(solution)/shard_map/psum | solution.py:255
  1457.4 135.8 %reduce-scatter.63.cloned.1.call-start = ((), (), s32[]{:S(2)}) async-start(), calls=%async_computation.43 | async-start | bytes 2654208
  (117 other events, 6011.5 us)
Sparse Core Ops, SparseCore 0:
  10.2 58.6 all-gather.28
  90.1 75.2 reduce-scatter.48
  168.2 53.4 all-gather.30
  244.3 21.1 all-gather.46
  271.2 78.6 reduce-scatter.50
  352.6 54.8 all-gather.32
  423.9 76.5 reduce-scatter.52
  503.3 53.4 all-gather.34
  579.0 21.1 all-gather.50
  608.4 78.6 reduce-scatter.54
  689.8 53.4 all-gather.36
  756.3 74.4 reduce-scatter.56
  859.7 53.4 all-gather.38
  953.7 74.5 reduce-scatter.58
  1055.4 53.4 all-gather.40
  1121.8 74.3 reduce-scatter.60
  1223.6 53.4 all-gather.42
  1300.3 21.0 reduce-scatter.46
  1346.0 20.0 reduce-scatter.34
  1369.1 21.2 reduce-scatter.40
  1392.8 21.1 reduce-scatter.44
  1437.2 20.0 reduce-scatter.32
  1460.2 52.5 all-reduce.7
  1516.5 76.6 reduce-scatter.62
  (5 shorter events, 91.5 us)
where the time goes:
time: 1690 us; the launch traced here: 1680 us
  waiting for transfers between devices  1080 us (64%)
  blocking collectives  331 us (20%)
  matrix products  124 us (7%)
  other arithmetic  64.9 us (4%)
  local copies, waits for them, and re-layouts  59.7 us (4%)
    unnamed x37, waiting for transfers between devices  607 us
    all_gather x4, waiting for transfers between devices, spread_grad(): return lax.all_gather(grad_low, 'col', axis=1, tiled=True)  188 us
    psum x4, blocking collectives, norm_backward(): lax.psum((jnp.sum(scaled_output, axis=1, keepdims=True), jnp.sum(scaled_o...  87.5 us
    all_gather x4, blocking collectives, normalize(): lax.all_gather(gain.astype(jnp.bfloat16), 'col', axis=0, tiled=True)  86 us
    all_gather x4, blocking collectives, normalize(): lax.all_gather(shift.astype(jnp.bfloat16), 'col', axis=0, tiled=True)  72.4 us
    psum x1, blocking collectives, backward_layer(): lax.psum((jnp.stack([gain_one, gain_two]), jnp.stack([shift_one, shift_tw...  52.9 us
    psum x1, waiting for transfers between devices, backward_layer(): lax.psum(summed[0].astype(jnp.bfloat16), 'dp').astype(jnp.float32)  48.5 us
    unnamed x241, local copies, waits for them, and re-layouts  48.2 us
  transfers between devices with their start and end apart: 29, of which 27 were waited for; matrix products, arithmetic and copies ran while one was open for 6% of the time, Pallas kernels for 0%

commit v1 on v0

v1 whole, which is shorter than its diff:
```python
import functools

import jax
import jax.numpy as jnp
from jax import lax
from jax.experimental import pallas as pl
from jax.experimental.pallas import tpu as pltpu
from jax.sharding import Mesh, PartitionSpec as P

WIDTH = 1024
HALF = WIDTH // 2
SEQ = 1025
LAYERS = 2
REAL = 128
ROWS = 144
OWN = 4 * ROWS
KEYS = 2 * OWN
QROWS = 640
CHUNKS = ((0, 256), (256, 256), (512, 128))
EPS = 1e-06
ROOT_HALF = 0.7071067811865476
INV_ROOT_TWO_PI = 0.3989422804014327
MESH = pl.DeviceIdType.MESH
AXES = ("x", "yl", "co", "yh", "z")
VM = pl.BlockSpec(memory_space=pltpu.VMEM)
F32 = jnp.float32
BF16 = jnp.bfloat16


def gelu_value(value):
    return 0.5 * value * (1.0 + lax.erf(value * ROOT_HALF))


def gelu_slope(value):
    return 0.5 * (1.0 + lax.erf(value * ROOT_HALF)) + value * INV_ROOT_TWO_PI * jnp.exp(
        -0.5 * value * value
    )


def dot_nt(left, right):
    return lax.dot_general(left, right, (((1,), (1,)), ((), ())), preferred_element_type=F32)


def dot_tn(left, right):
    return lax.dot_general(left, right, (((0,), (0,)), ((), ())), preferred_element_type=F32)


def dot_nn(left, right):
    return jnp.dot(left, right, preferred_element_type=F32)


def device(**moved):
    return tuple(moved[a] if a in moved else lax.axis_index(a) for a in AXES)


def remote(src, dst, send, recv, to):
    return pltpu.make_async_remote_copy(
        src_ref=src, dst_ref=dst, send_sem=send, recv_sem=recv, device_id=to, device_id_type=MESH
    )


def signal(to):
    pl.semaphore_signal(
        pltpu.get_barrier_semaphore(), inc=1, device_id=to, device_id_type=MESH
    )


def ring():
    z = lax.axis_index("z")
    right, left, across = lax.rem(z + 1, 4), lax.rem(z + 3, 4), lax.rem(z + 2, 4)
    return z, right, left, across, device(z=right), device(z=left)


def greet_ring():
    _, _, _, _, to_right, to_left = ring()
    signal(to_right)
    signal(to_left)
    pl.semaphore_wait(pltpu.get_barrier_semaphore(), 2)


A = pl.ds(0, HALF)
B = pl.ds(HALF, HALF)


def ring_reduce(part, fin, relay, stage, send, recv):
    z, right, left, across, to_right, to_left = ring()

    def copy(i, src, dst, to):
        return remote(src, dst, send.at[i], recv.at[i], to)

    far_r = copy(0, part.at[across, :, A], relay.at[0], to_right)
    far_l = copy(1, part.at[across, :, B], relay.at[1], to_left)
    near_r = copy(2, part.at[right, :, B], fin.at[0, :, B], to_right)
    near_l = copy(3, part.at[left, :, A], fin.at[1, :, A], to_left)
    for c in (far_r, far_l, near_r, near_l):
        c.start()
    far_r.wait_recv()
    stage[0] = (part[right, :, A].astype(F32) + relay[0].astype(F32)).astype(BF16)
    sum_r = copy(4, stage.at[0], fin.at[0, :, A], to_right)
    sum_r.start()
    far_l.wait_recv()
    stage[1] = (part[left, :, B].astype(F32) + relay[1].astype(F32)).astype(BF16)
    sum_l = copy(5, stage.at[1], fin.at[1, :, B], to_left)
    sum_l.start()
    for c in (near_r, near_l, sum_r, sum_l):
        c.wait_recv()
    total = part[z].astype(F32) + fin[0].astype(F32) + fin[1].astype(F32)
    return total, (far_r, far_l, near_r, near_l, sum_r, sum_l)


def ring_gather(out, send, recv, base):
    z, right, left, across, to_right, to_left = ring()

    def copy(i, owner, cols, to):
        ref = out.at[owner, :, cols]
        return remote(ref, ref, send.at[base + i], recv.at[base + i], to)

    def lands(i, owner, cols):
        copy(i, owner, cols, to_right).wait_recv()

    first = (
        copy(0, z, A, to_right),
        copy(1, z, B, to_left),
        copy(2, z, B, to_right),
        copy(3, z, A, to_left),
    )
    for c in first:
        c.start()
    lands(0, left, A)
    on_r = copy(4, left, A, to_right)
    on_r.start()
    lands(1, right, B)
    on_l = copy(5, right, B, to_left)
    on_l.start()
    lands(2, left, B)
    lands(3, right, A)
    lands(4, across, A)
    lands(5, across, B)
    return first + (on_r, on_l)


def norm_of(value):
    mean = jnp.mean(value, axis=1, keepdims=True)
    meansq = jnp.mean(value * value, axis=1, keepdims=True)
    rstd = lax.rsqrt(meansq - mean * mean + EPS)
    return (value - mean) * rstd, rstd


def norm_back(grad, value, gain):
    hat, rstd = norm_of(value)
    e = grad * gain
    return (
        rstd
        * (
            e
            - jnp.mean(e, axis=1, keepdims=True)
            - hat * jnp.mean(e * hat, axis=1, keepdims=True)
        ),
        jnp.sum(grad * hat, axis=0, keepdims=True),
        jnp.sum(grad, axis=0, keepdims=True),
    )


RING_SCRATCH = [
    pltpu.VMEM((2, ROWS, WIDTH), BF16),
    pltpu.VMEM((2, ROWS, HALF), BF16),
    pltpu.VMEM((2, ROWS, HALF), BF16),
    pltpu.SemaphoreType.DMA((12,)),
    pltpu.SemaphoreType.DMA((12,)),
]
GAIN, SHIFT, BRANCH, SCALE = 0, 4, 8, 12


def call(kernel, outs, scratch, ident, inputs, **more):
    return pl.pallas_call(
        kernel,
        out_shape=[jax.ShapeDtypeStruct(s, d) for s, d in outs],
        in_specs=[VM] * len(inputs),
        out_specs=[VM] * len(outs),
        scratch_shapes=scratch,
        compiler_params=pltpu.CompilerParams(
            collective_id=ident, has_side_effects=True, vmem_limit_bytes=24 * 2**20
        ),
        **more,
    )(*inputs)


SHARD = (ROWS, WIDTH)
ALL = (4, ROWS, WIDTH)


def forward_kernel(
    at, part, x, table, branch_out, x_out, n_out, fin, relay, stage, send, recv
):
    greet_ring()
    total, sent = ring_reduce(part, fin, relay, stage, send, recv)
    bias, scale, gain, shift = (table[r : r + 1, :] for r in at)
    branch = total + bias
    x_new = x[...] + scale * branch
    branch_out[...] = branch
    x_out[...] = x_new
    hat, _ = norm_of(x_new)
    n_out[lax.axis_index("z")] = (hat * gain + shift).astype(BF16)
    for c in sent + ring_gather(n_out, send, recv, 6):
        c.wait_send()


def forward_step(part, x, table, at, ident):
    return call(
        functools.partial(forward_kernel, at),
        [(SHARD, F32), (SHARD, F32), (ALL, BF16)],
        RING_SCRATCH,
        ident,
        (part, x, table),
    )


def turn_kernel(at, part, x, cot, table, x_out, sums, d_out, fin, relay, stage, send, recv):
    greet_ring()
    bias, scale = (table[r : r + 1, :] for r in at)
    df = (cot[...] * scale).astype(BF16)
    d_out[lax.axis_index("z")] = df
    total, sent = ring_reduce(part, fin, relay, stage, send, recv)
    branch = total + bias
    x_out[...] = x[...] + scale * branch
    sums[...] = jnp.zeros_like(sums)
    sums[2:3, :] = jnp.sum(cot[...] * branch, axis=0, keepdims=True)
    sums[3:4, :] = jnp.sum(df.astype(F32), axis=0, keepdims=True)
    for c in sent + ring_gather(d_out, send, recv, 6):
        c.wait_send()


def turn_step(part, x, cot, table, at, ident):
    return call(
        functools.partial(turn_kernel, at),
        [(SHARD, F32), ((8, WIDTH), F32), (ALL, BF16)],
        RING_SCRATCH,
        ident,
        (part, x, cot, table),
    )


def backward_kernel(
    at, part, value, dx, branch, table, dx_out, sums, d_out, fin, relay, stage, send, recv
):
    greet_ring()
    total, sent = ring_reduce(part, fin, relay, stage, send, recv)
    gain, scale = (table[r : r + 1, :] for r in at)
    dr, gain_sum, shift_sum = norm_back(total, value[...], gain)
    dx_new = dx[...] + dr
    dx_out[...] = dx_new
    df = (dx_new * scale).astype(BF16)
    d_out[lax.axis_index("z")] = df
    sums[...] = jnp.zeros_like(sums)
    sums[0:1, :] = gain_sum
    sums[1:2, :] = shift_sum
    sums[2:3, :] = jnp.sum(dx_new * branch[...], axis=0, keepdims=True)
    sums[3:4, :] = jnp.sum(df.astype(F32), axis=0, keepdims=True)
    for c in sent + ring_gather(d_out, send, recv, 6):
        c.wait_send()


def backward_step(part, value, dx, branch, table, at, ident):
    return call(
        functools.partial(backward_kernel, at),
        [(SHARD, F32), ((8, WIDTH), F32), (ALL, BF16)],
        RING_SCRATCH,
        ident,
        (part, value, dx, branch, table),
    )


def cols(q):
    return pl.ds(q * 128, 128)


def first_kernel(
    pieces, pack, x_out, cot_out, n_out, pack_out, landed, psend, precv, ksend, krecv, send, recv
):
    x_, yl, co, yh, z = (lax.axis_index(a) for a in AXES)
    me = yh * 4 + z
    home = yh == co
    for j in range(8):
        to = device(yh=j // 4, z=j % 4)

        @pl.when(me != j)
        def _():
            signal(to)

        mine = home & (me == j)

        @pl.when(jnp.logical_not(mine))
        def _():
            signal(device(yh=j // 4, z=j % 4, co=yh))

    barrier = pltpu.get_barrier_semaphore()

    @pl.when(home)
    def _():
        pl.semaphore_wait(barrier, 14)

    @pl.when(jnp.logical_not(home))
    def _():
        pl.semaphore_wait(barrier, 15)

    def piece(j):
        src = pieces.at[:, pl.ds(j * REAL, ROWS), :]
        dst = landed.at[:, :, pl.ds(pl.multiple_of(me * 128, 128), 128)]
        to = device(yh=co, co=j // 4, z=j % 4)
        there = remote(src, dst, psend.at[j], precv.at[me], to)
        here = pltpu.make_async_copy(src, dst, precv.at[me])
        return there, here, home & (co * 4 + z == j)

    def note(j):
        return remote(
            pack, pack_out.at[me], ksend.at[j], krecv.at[me], device(yh=j // 4, z=j % 4)
        )

    pack_out[me] = pack[...]
    for j in range(8):
        there, here, own = piece(j)

        @pl.when(own)
        def _():
            here.start()

        @pl.when(jnp.logical_not(own))
        def _():
            there.start()

    for j in range(8):

        @pl.when(me != j)
        def _():
            note(j).start()

    for q in range(8):
        dst = landed.at[:, :, cols(q)]
        got = remote(dst, dst, psend.at[q], precv.at[q], device(z=lax.rem(z + 1, 4)))
        own = home & (me == q)

        @pl.when(own)
        def _():
            pltpu.make_async_copy(dst, dst, precv.at[q]).wait()

        @pl.when(jnp.logical_not(own))
        def _():
            got.wait_recv()

        @pl.when(me != q)
        def _():
            remote(
                pack, pack_out.at[q], ksend.at[q], krecv.at[q], device(z=lax.rem(z + 1, 4))
            ).wait_recv()

    value = landed[0].astype(F32)
    x_out[...] = value
    row = lax.broadcasted_iota(jnp.int32, (ROWS, 1), 0)
    last = jnp.where((co == 1) & (z == 3), REAL + 1, REAL)
    cot_out[...] = jnp.where(row < last, landed[1].astype(F32), 0.0)
    gain = jnp.concatenate([pack_out[q, GAIN : GAIN + 1, :] for q in range(8)], axis=1)
    shift = jnp.concatenate([pack_out[q, SHIFT : SHIFT + 1, :] for q in range(8)], axis=1)
    hat, _ = norm_of(value)
    n_out[z] = (hat * gain + shift).astype(BF16)
    for c in ring_gather(n_out, send, recv, 0):
        c.wait_send()
    for j in range(8):
        there, here, own = piece(j)

        @pl.when(jnp.logical_not(own))
        def _():
            there.wait_send()

        @pl.when(me != j)
        def _():
            note(j).wait_send()


def first_step(pieces, pack, ident):
    return call(
        first_kernel,
        [(SHARD, F32), (SHARD, F32), (ALL, BF16), ((8, 32, 128), F32)],
        [
            pltpu.VMEM((2, ROWS, WIDTH), BF16),
            pltpu.SemaphoreType.DMA((8,)),
            pltpu.SemaphoreType.DMA((8,)),
            pltpu.SemaphoreType.DMA((8,)),
            pltpu.SemaphoreType.DMA((8,)),
            pltpu.SemaphoreType.DMA((6,)),
            pltpu.SemaphoreType.DMA((6,)),
        ],
        ident,
        (pieces, pack),
    )


def last_kernel(
    at,
    part,
    value,
    dx,
    x_end,
    table,
    landed,
    sums,
    both,
    fin,
    relay,
    stage,
    send,
    recv,
    psend,
    precv,
):
    x_, yl, co, yh, z = (lax.axis_index(a) for a in AXES)
    shard = co * 4 + z
    home = yh == co
    greeted = 0
    _, _, _, _, to_right, to_left = ring()
    signal(to_right)
    signal(to_left)
    for s in range(8):

        @pl.when(jnp.logical_not(home & (shard == s)))
        def _():
            signal(device(yh=co, co=s // 4, z=s % 4))

    barrier = pltpu.get_barrier_semaphore()

    @pl.when(home)
    def _():
        pl.semaphore_wait(barrier, 9)

    @pl.when(jnp.logical_not(home))
    def _():
        pl.semaphore_wait(barrier, 10)

    def piece(k, q):
        src = both.at[k, :, cols(q)]
        dst = landed.at[k, shard]
        to = device(co=yh, yh=q // 4, z=q % 4)
        there = remote(src, dst, psend.at[k, q], precv.at[k, shard], to)
        here = pltpu.make_async_copy(src, dst, precv.at[k, shard])
        return there, here, home & (yh * 4 + z == q)

    def send_all(k):
        for q in range(8):
            there, here, own = piece(k, q)

            @pl.when(own)
            def _():
                here.start()

            @pl.when(jnp.logical_not(own))
            def _():
                there.start()

    both[0] = x_end[...].astype(BF16)
    send_all(0)
    total, sent = ring_reduce(part, fin, relay, stage, send, recv)
    (gain,) = (table[r : r + 1, :] for r in at)
    dr, gain_sum, shift_sum = norm_back(total, value[...], gain)
    both[1] = (dx[...] + dr).astype(BF16)
    send_all(1)
    sums[...] = jnp.zeros_like(sums)
    sums[0:1, :] = gain_sum
    sums[1:2, :] = shift_sum
    for c in sent:
        c.wait_send()
    for k in range(2):
        for s in range(8):
            dst = landed.at[k, s]
            got = remote(dst, dst, psend.at[k, s], precv.at[k, s], to_right)
            own = home & (shard == s)

            @pl.when(own)
            def _():
                pltpu.make_async_copy(dst, dst, precv.at[k, s]).wait()

            @pl.when(jnp.logical_not(own))
            def _():
                got.wait_recv()

            there, here, mine = piece(k, s)

            @pl.when(jnp.logical_not(mine))
            def _():
                there.wait_send()


def last_step(part, value, dx, x_end, table, at, ident):
    return call(
        functools.partial(last_kernel, at),
        [((2, 8, ROWS, 128), BF16), ((8, WIDTH), F32)],
        [pltpu.VMEM((2,) + SHARD, BF16)]
        + RING_SCRATCH
        + [pltpu.SemaphoreType.DMA((2, 8)), pltpu.SemaphoreType.DMA((2, 8))],
        ident,
        (part, value, dx, x_end, table),
    )


def swap_kernel(own, other, send, recv):
    co = lax.axis_index("co")
    to = device(co=1 - co)
    signal(to)
    pl.semaphore_wait(pltpu.get_barrier_semaphore(), 1)
    c = remote(own, other, send, recv, to)
    c.start()
    c.wait()


def swap(own, ident):
    return call(
        swap_kernel,
        [(own.shape, own.dtype)],
        [pltpu.SemaphoreType.DMA, pltpu.SemaphoreType.DMA],
        ident,
        (own,),
    )[0]


def lane_heads(value):
    lane = lax.broadcasted_iota(jnp.int32, value.shape, 1)
    zero = jnp.zeros_like(value)
    return jnp.where(lane < 64, value, zero), jnp.where(lane < 64, zero, value)


def attend_kernel(q, k, v, ko, vo, mask, att, lse, kall, vt, qpad, ot):
    kall[0:OWN] = k[...]
    kall[OWN:KEYS] = ko[...]
    vt[:, 0:OWN] = v[...].T
    vt[:, OWN:KEYS] = vo[...].T
    for hh, qh in enumerate(lane_heads(q[...] * 0.125)):
        qpad[hh, 0:OWN] = qh
        qpad[hh, OWN:QROWS] = jnp.zeros((QROWS - OWN, 128), BF16)
    lse[...] = jnp.zeros_like(lse)
    for hh in range(2):
        for lo, n in CHUNKS:
            bias = mask[...] if n == 128 else jnp.concatenate([mask[...]] * 2, axis=1)
            s = dot_nt(kall[...], qpad[hh, lo : lo + n]) + bias
            top = jnp.max(s, axis=0, keepdims=True)
            e = jnp.exp(s - top)
            total = jnp.sum(e, axis=0, keepdims=True)
            p = (e * (1.0 / total)).astype(BF16)
            ot[hh * 64 : hh * 64 + 64, lo : lo + n] = dot_nn(vt[hh * 64 : hh * 64 + 64], p)
            lse[hh : hh + 1, lo : lo + n] = top + jnp.log(total)
    att[...] = ot[...].T[0:OWN].astype(BF16)


def attend(qkv, other, mask):
    def block(f):
        return pl.BlockSpec((OWN, 128), lambda h: (0, f(h)))

    return pl.pallas_call(
        attend_kernel,
        grid=(2,),
        out_shape=[
            jax.ShapeDtypeStruct((OWN, 256), BF16),
            jax.ShapeDtypeStruct((2, 8, QROWS), F32),
        ],
        in_specs=[
            block(lambda h: 3 * h),
            block(lambda h: 3 * h + 1),
            block(lambda h: 3 * h + 2),
            block(lambda h: 2 * h),
            block(lambda h: 2 * h + 1),
            pl.BlockSpec((KEYS, 128), lambda h: (0, 0)),
        ],
        out_specs=[
            block(lambda h: h),
            pl.BlockSpec((None, 8, QROWS), lambda h: (h, 0, 0)),
        ],
        scratch_shapes=[
            pltpu.VMEM((KEYS, 128), BF16),
            pltpu.VMEM((128, KEYS), BF16),
            pltpu.VMEM((2, QROWS, 128), BF16),
            pltpu.VMEM((128, QROWS), F32),
        ],
        compiler_params=pltpu.CompilerParams(vmem_limit_bytes=40 * 2**20),
    )(qkv, qkv, qkv, other, other, mask)


def attend_back_kernel(
    q, k, v, ko, vo, do, lse, mask, dq, own, oth, kall, vall, kt, qpad, dpad, dqt, dk, dv
):
    kall[0:OWN] = k[...]
    kall[OWN:KEYS] = ko[...]
    vall[0:OWN] = v[...]
    vall[OWN:KEYS] = vo[...]
    kt[:, 0:OWN] = k[...].T
    kt[:, OWN:KEYS] = ko[...].T
    for hh, (qh, dh) in enumerate(zip(lane_heads(q[...] * 0.125), lane_heads(do[...]))):
        qpad[hh, 0:OWN] = qh
        qpad[hh, OWN:QROWS] = jnp.zeros((QROWS - OWN, 128), BF16)
        dpad[hh, 0:OWN] = dh
        dpad[hh, OWN:QROWS] = jnp.zeros((QROWS - OWN, 128), BF16)
    dk[...] = jnp.zeros_like(dk)
    dv[...] = jnp.zeros_like(dv)
    for hh in range(2):
        for lo, n in CHUNKS:
            bias = mask[...] if n == 128 else jnp.concatenate([mask[...]] * 2, axis=1)
            qc = qpad[hh, lo : lo + n]
            dc = dpad[hh, lo : lo + n]
            s = dot_nt(kall[...], qc) + bias
            p = jnp.exp(s - lse[hh : hh + 1, lo : lo + n])
            dp = dot_nt(vall[...], dc)
            delta = jnp.sum(p * dp, axis=0, keepdims=True)
            ds = (p * (dp - delta)).astype(BF16)
            dv[...] += dot_nn(p.astype(BF16), dc)
            dk[...] += dot_nn(ds, qc)
            dqt[hh * 64 : hh * 64 + 64, lo : lo + n] = dot_nn(kt[hh * 64 : hh * 64 + 64], ds)
    dq[...] = (dqt[...].T[0:OWN] * 0.125).astype(BF16)
    own[:, 0:128] = dk[0:OWN]
    own[:, 128:256] = dv[0:OWN]
    oth[:, 0:128] = dk[OWN:KEYS].astype(BF16)
    oth[:, 128:256] = dv[OWN:KEYS].astype(BF16)


def attend_back(qkv, other, datt, lse, mask):
    def block(f):
        return pl.BlockSpec((OWN, 128), lambda h: (0, f(h)))

    wide = pl.BlockSpec((OWN, 256), lambda h: (0, h))
    return pl.pallas_call(
        attend_back_kernel,
        grid=(2,),
        out_shape=[
            jax.ShapeDtypeStruct((OWN, 256), BF16),
            jax.ShapeDtypeStruct((OWN, 512), F32),
            jax.ShapeDtypeStruct((OWN, 512), BF16),
        ],
        in_specs=[
            block(lambda h: 3 * h),
            block(lambda h: 3 * h + 1),
            block(lambda h: 3 * h + 2),
            block(lambda h: 2 * h),
            block(lambda h: 2 * h + 1),
            block(lambda h: h),
            pl.BlockSpec((None, 8, QROWS), lambda h: (h, 0, 0)),
            pl.BlockSpec((KEYS, 128), lambda h: (0, 0)),
        ],
        out_specs=[block(lambda h: h), wide, wide],
        scratch_shapes=[
            pltpu.VMEM((KEYS, 128), BF16),
            pltpu.VMEM((KEYS, 128), BF16),
            pltpu.VMEM((128, KEYS), BF16),
            pltpu.VMEM((2, QROWS, 128), BF16),
            pltpu.VMEM((2, QROWS, 128), BF16),
            pltpu.VMEM((128, QROWS), F32),
            pltpu.VMEM((KEYS, 128), F32),
            pltpu.VMEM((KEYS, 128), F32),
        ],
        compiler_params=pltpu.CompilerParams(vmem_limit_bytes=48 * 2**20),
    )(qkv, qkv, qkv, other, other, datt, lse, mask)


ROW8 = ("yl", "co", "yh")


def gather_weight(shard, side):
    stacked = lax.all_gather(shard, ROW8).reshape((4, 2) + shard.shape)
    if side == 0:
        moved = stacked.transpose(0, 2, 1, 3)
        return moved.reshape(4 * shard.shape[0], 2 * shard.shape[1])
    return stacked.transpose(1, 2, 0, 3).reshape(2 * shard.shape[0], 4 * shard.shape[1])


def reduce_weight(part, side):
    rows, columns = part.shape
    if side == 0:
        blocks = part.reshape(4, rows // 4, 2, columns // 2).transpose(0, 2, 1, 3)
    else:
        blocks = part.reshape(2, rows // 2, 4, columns // 4).transpose(2, 0, 1, 3)
    blocks = blocks.reshape((8,) + blocks.shape[2:]).astype(BF16)
    mine = lax.psum_scatter(blocks, ROW8, scatter_dimension=0, tiled=False)
    return lax.psum(mine, "x").astype(F32)


def on_device(
    tokens,
    cotangent,
    attend_weight,
    output_weight,
    up_weight,
    down_weight,
    norm_gain,
    norm_shift,
    attend_bias,
    branch_bias,
    layer_scale,
    hidden_bias,
):
    co, yh, z = (lax.axis_index(a) for a in ("co", "yh", "z"))
    weights = [
        (
            gather_weight(attend_weight[l].reshape(256, 384), 0),
            gather_weight(output_weight[l], 1),
            gather_weight(up_weight[l], 0),
            gather_weight(down_weight[l], 1),
        )
        for l in range(LAYERS)
    ]
    pieces = jnp.pad(jnp.stack([tokens, cotangent.astype(BF16)]), ((0, 0), (0, 15), (0, 0)))
    pack = jnp.concatenate(
        [
            norm_gain.reshape(4, 128),
            norm_shift.reshape(4, 128),
            branch_bias.reshape(4, 128),
            layer_scale.reshape(4, 128),
            attend_bias.reshape(4, 128),
            hidden_bias.reshape(8, 128),
            jnp.zeros((4, 128), F32),
        ]
    )
    ident = iter(range(40))
    x, cot, n_all, packs = first_step(pieces, pack, next(ident))
    table = packs[:, 0:16].transpose(1, 0, 2).reshape(16, WIDTH)
    here = jnp.stack(
        [
            lax.dynamic_index_in_dim(packs, z, keepdims=False),
            lax.dynamic_index_in_dim(packs, z + 4, keepdims=False),
        ]
    )
    row = jnp.arange(OWN)
    block, inside = row // ROWS, row % ROWS

    def hidden_keys(half):
        real = (inside < REAL) | ((inside == REAL) & (block == 3) & (half == 1))
        return jnp.where(real, 0.0, -1e30).astype(F32)

    mask = jnp.concatenate([hidden_keys(co), hidden_keys(1 - co)])
    mask = jnp.broadcast_to(mask[:, None], (KEYS, 128))

    saved = []
    for l in range(LAYERS):
        wqkv, wout, wup, wdown = weights[l]
        ab = here[:, 16 + 2 * l : 18 + 2 * l]
        qkv_bias = jnp.concatenate(
            [ab[0, 0], jnp.zeros(128), ab[0, 1], ab[1, 0], jnp.zeros(128), ab[1, 1]]
        )
        n1 = n_all.reshape(OWN, WIDTH)
        qkv = (dot_nn(n1, wqkv) + qkv_bias).astype(BF16)
        kv = jnp.concatenate([qkv[:, 128:384], qkv[:, 512:768]], axis=1)
        other = swap(kv, next(ident))
        att, lse = attend(qkv, other, mask)
        part = dot_nn(att, wout).astype(BF16).reshape(ALL)
        at = (BRANCH + 2 * l, SCALE + 2 * l, GAIN + 2 * l + 1, SHIFT + 2 * l + 1)
        a, m, n_all = forward_step(part, x, table, at, next(ident))
        n2 = n_all.reshape(OWN, WIDTH)
        hb = here[:, 20 + 4 * l : 24 + 4 * l].reshape(WIDTH)
        u = dot_nn(n2, wup) + hb
        g = gelu_value(u).astype(BF16)
        part = dot_nn(g, wdown).astype(BF16).reshape(ALL)
        saved.append([x, n1, qkv, other, att, lse, a, m, n2, u, g])
        if l + 1 < LAYERS:
            at = (BRANCH + 2 * l + 1, SCALE + 2 * l + 1, GAIN + 2 * l + 2, SHIFT + 2 * l + 2)
            f, x, n_all = forward_step(part, m, table, at, next(ident))
            saved[l].append(f)
        else:
            at = (BRANCH + 2 * l + 1, SCALE + 2 * l + 1)
            x_end, sums, d_all = turn_step(part, m, cot, table, at, next(ident))

    gain_sums, shift_sums, scale_sums, branch_sums = ([None] * 4 for _ in range(4))
    scale_sums[3], branch_sums[3] = sums[2], sums[3]
    hidden_sums, qkv_sums, grads = [None] * LAYERS, [None] * LAYERS, [None] * LAYERS
    dx = cot
    for l in reversed(range(LAYERS)):
        wqkv, wout, wup, wdown = weights[l]
        x, n1, qkv, other, att, lse, a, m, n2, u, g = saved[l][:11]
        df = d_all.reshape(OWN, WIDTH)
        du = (dot_nt(df, wdown) * gelu_slope(u)).astype(BF16)
        part = dot_nt(du, wup).astype(BF16).reshape(ALL)
        hidden_sums[l] = jnp.sum(du.astype(F32), axis=0)
        at = (GAIN + 2 * l + 1, SCALE + 2 * l)
        dm, sums, d_all = backward_step(part, m, dx, a, table, at, next(ident))
        gain_sums[2 * l + 1], shift_sums[2 * l + 1] = sums[0], sums[1]
        scale_sums[2 * l], branch_sums[2 * l] = sums[2], sums[3]
        down_grad = reduce_weight(dot_tn(g, df), 1)
        up_grad = reduce_weight(dot_tn(n2, du), 0)
        da = d_all.reshape(OWN, WIDTH)
        datt = dot_nt(da, wout).astype(BF16)
        output_grad = reduce_weight(dot_tn(att, da), 1)
        dq, own, oth = attend_back(qkv, other, datt, lse, mask)
        dkv = (own + swap(oth, next(ident)).astype(F32)).astype(BF16)
        dqkv = jnp.concatenate(
            [dq[:, 0:128], dkv[:, 0:256], dq[:, 128:256], dkv[:, 256:512]], axis=1
        )
        qkv_sums[l] = jnp.sum(dqkv.astype(F32), axis=0)
        part = dot_nt(dqkv, wqkv).astype(BF16).reshape(ALL)
        attend_grad = reduce_weight(dot_tn(n1, dqkv), 0)
        if l > 0:
            at = (GAIN + 2 * l, SCALE + 2 * l - 1)
            dx, sums, d_all = backward_step(
                part, x, dm, saved[l - 1][11], table, at, next(ident)
            )
            scale_sums[2 * l - 1], branch_sums[2 * l - 1] = sums[2], sums[3]
        else:
            landed, sums = last_step(part, x, dm, x_end, table, (GAIN + 2 * l,), next(ident))
        gain_sums[2 * l], shift_sums[2 * l] = sums[0], sums[1]
        grads[l] = (attend_grad.reshape(256, 3, 128), output_grad, up_grad, down_grad)

    everywhere = jnp.stack(gain_sums + shift_sums + branch_sums + scale_sums)
    everywhere = lax.psum(everywhere, "z")
    everywhere = everywhere.reshape(16, 2, 4, 128)
    everywhere = lax.dynamic_index_in_dim(everywhere, z, axis=2, keepdims=False)
    ringed = jnp.concatenate(
        [
            everywhere.transpose(1, 0, 2),
            jnp.stack(qkv_sums).reshape(2, 2, 3, 128).transpose(1, 0, 2, 3).reshape(2, 6, 128),
            jnp.stack(hidden_sums).reshape(2, 2, 4, 128).transpose(1, 0, 2, 3).reshape(2, 8, 128),
        ],
        axis=1,
    )
    small = lax.psum(ringed, ("x", "yl", "co", "yh"))
    small = lax.dynamic_index_in_dim(small, yh, keepdims=False)
    bias_grad = small[16:22].reshape(2, 3, 128)[:, 0::2]

    def rows(k):
        return jnp.concatenate(
            [landed[k, 0:7, 0:REAL].reshape(7 * REAL, 128), landed[k, 7, 0 : REAL + 1]]
        ).astype(F32)

    return (
        rows(0),
        rows(1),
        jnp.stack([grads[l][0] for l in range(LAYERS)]),
        jnp.stack([grads[l][1] for l in range(LAYERS)]),
        jnp.stack([grads[l][2] for l in range(LAYERS)]),
        jnp.stack([grads[l][3] for l in range(LAYERS)]),
        small[0:4].reshape(2, 2, 128),
        small[4:8].reshape(2, 2, 128),
        bias_grad,
        small[8:12].reshape(2, 2, 128),
        small[12:16].reshape(2, 2, 128),
        small[22:30].reshape(2, 512),
    )


def solution(mesh):
    split = Mesh(mesh.devices.reshape(4, 2, 2, 2, 4), AXES)
    images, row, col = ("x", "yl", "co"), ("yl", "co"), ("yh", "z")
    placed = (
        P(images, col),
        P(images, col),
        P(None, row, None, col),
        P(None, col, row),
        P(None, row, col),
        P(None, col, row),
        P(None, None, col),
        P(None, None, col),
        P(None, None, col),
        P(None, None, col),
        P(None, None, col),
        P(None, col),
    )
    return jax.shard_map(
        on_device, mesh=split, in_specs=placed, out_specs=placed, check_vma=False
    )
```

time: 1690 us -> 1130 us (0.67)
  waiting for transfers between devices: 1080 us -> 468 us
  Pallas kernels: 0 us -> 287 us
  blocking collectives: 331 us -> 200 us
  matrix products: 124 us -> 53.5 us
  other arithmetic: 64.9 us -> 15.1 us
  local copies, waits for them, and re-layouts: 59.7 us -> 87.3 us
    unnamed x37 -> x16, waiting for transfers between devices: 607 us -> 1.28 us
    pallas_call x0 -> x17, Pallas kernels: none -> 287 us  [the longest x13 243 us: call(): pl.pallas_call(kernel, out_shape=[jax.ShapeDtypeStruct(s, d) for s, d in...]
    all_gather x12 -> x6, waiting for transfers between devices: 289 us -> 146 us  [gather_weight(): stacked = lax.all_gather(shard, ROW8).reshape((4, 2) + shard.shape)]
    reduce_scatter x8, waiting for transfers between devices: 139 us -> 280 us  [reduce_weight(): mine = lax.psum_scatter(blocks, ROW8, scatter_dimension=0, tiled=False)]
    all_gather x12 -> x2, blocking collectives: 191 us -> 73 us  [gather_weight(): stacked = lax.all_gather(shard, ROW8).reshape((4, 2) + shard.shape)]
    dot_general x36 -> x24, matrix products: 124 us -> 53.5 us  [the longest x8 25.4 us: dot_tn(): lax.dot_general(left, right, (((0,), (0,)), ((), ())), preferred_element_...]
    reduce_sum x19 -> x2, other arithmetic: 28 us -> 0.42 us  [on_device(): qkv_sums[l] = jnp.sum(dqkv.astype(F32), axis=0)]
    reshape x0 -> x15, local copies, waits for them, and re-layouts: none -> 22.4 us  [the longest x8 21.1 us: gather_weight(): stacked = lax.all_gather(shard, ROW8).reshape((4, 2) + shard.shape)]
  transfers between devices with their start and end apart: 29 -> 16, of which waited for: 27 -> 10; matrix products, arithmetic and copies ran while one was open for 6% -> 10% of each run, Pallas kernels for 0% -> 18%
where the time goes in v1:
time: 1130 us
  waiting for transfers between devices  468 us (41%)
  Pallas kernels  287 us (25%)
  blocking collectives  200 us (18%)
  local copies, waits for them, and re-layouts  87.3 us (8%)
  matrix products  53.5 us (5%)
  between operations  15.7 us (1%)
  other arithmetic  15.1 us (1%)
    reduce_scatter x8, waiting for transfers between devices, reduce_weight(): mine = lax.psum_scatter(blocks, ROW8, scatter_dimension=0, tiled=False)  280 us
    pallas_call x13, Pallas kernels, call(): pl.pallas_call(kernel, out_shape=[jax.ShapeDtypeStruct(s, d) for s, d in...  243 us
    all_gather x6, waiting for transfers between devices, gather_weight(): stacked = lax.all_gather(shard, ROW8).reshape((4, 2) + shard.shape)  146 us
    psum x1, blocking collectives, on_device(): small = lax.psum(ringed, ('x', 'yl', 'co', 'yh'))  127 us
    all_gather x2, blocking collectives, gather_weight(): stacked = lax.all_gather(shard, ROW8).reshape((4, 2) + shard.shape)  73 us
    psum x1, waiting for transfers between devices, on_device(): everywhere = lax.psum(everywhere, 'z')  40.5 us
    unnamed x179, local copies, waits for them, and re-layouts  27.5 us
    dot_general x8, matrix products, dot_tn(): lax.dot_general(left, right, (((0,), (0,)), ((), ())), preferred_element_...  25.4 us
  transfers between devices with their start and end apart: 16, of which 10 were waited for; matrix products, arithmetic and copies ran while one was open for 10% of the time, Pallas kernels for 18%

profile of v1, /device:TPU:0, one launch (start us, length us, event | category | flops | bytes accessed | tf_op | source)
XLA Modules:
  0.0 1126.7 jit_solution(7494564593122905306)
XLA Ops:
  13.6 44.9 %all_gather.25 = bf16[8,128,256]{2,1,0:T(8,128)(2,1)S(1)} all-gather(bf16[1,128,256]{2,1,0:T(8,128)(2,1)S(1)} %get-tuple-element.153), channel_id=1, replica_groups=mesh['x'=4,'yl'=2,'co'=2,'yh'=2,'z'=4] {'yl','co','yh'}, dimensions={0}, use_global_device_ids=true | all-gather | bytes 589824 | tf_op jit(solution)/shard_map/all_gather | solution.py:662
  59.9 28.0 %all_gather.29 = bf16[8,128,256]{2,1,0:T(8,128)(2,1)S(1)} all-gather(bf16[1,128,256]{2,1,0:T(8,128)(2,1)S(1)} %get-tuple-element.152), channel_id=1, replica_groups=mesh['x'=4,'yl'=2,'co'=2,'yh'=2,'z'=4] {'yl','co','yh'}, dimensions={0}, use_global_device_ids=true | all-gather | bytes 589824 | tf_op jit(solution)/shard_map/all_gather | solution.py:662
  89.4 40.9 %shard_map.211 = (f32[144,1024]{1,0:T(8,128)S(1)}, f32[144,1024]{1,0:T(8,128)S(1)}, bf16[4,144,1024]{2,1,0:T(8,128)(2,1)S(1)}, f32[8,32,128]{2,1,0:T(8,128)S(1)}) custom-call(bf16[2,1040,128]{2,1,0:T(8,128)(2,1)S(1)} %fusion.50.pieces, f32[32,128]{1,0:T(8,128)S(1)} %concatenate.35.pack), custom_call_target="tpu_custom_call" | custom-call | tf_op jit(solution)/shard_map/pallas_call | solution.py:175
  156.0 24.8 %shard_map.214 = (f32[144,1024]{1,0:T(8,128)S(1)}, f32[144,1024]{1,0:T(8,128)S(1)}, bf16[4,144,1024]{2,1,0:T(8,128)(2,1)S(1)}) custom-call(bf16[4,144,1024]{2,1,0:T(8,128)(2,1)S(1)} %bitcast.326, f32[144,1024]{1,0:T(8,128)S(1)} %get-tuple-element.52.x.value, f32[16,1024]{1,0:T(8,128)S(1)} %copy_bitcast_fusion.table), custom_call_target="tpu_custom_call" | custom-call | tf_op jit(solution)/shard_map/pallas_call | solution.py:175
  182.7 20.0 %all-gather.9.cloned.1.call-done = bf16[8,256,512]{2,1,0:T(8,128)(2,1)} async-done(((bf16[1,256,512]{2,1,0:T(8,128)(2,1)}), bf16[8,256,512]{2,1,0:T(8,128)(2,1)}) %all-gather.9.cloned.1.call-update) | async-done | bytes 2097168 | tf_op jit(solution)/shard_map/all_gather | solution.py:662
  208.4 55.5 %all-gather.11.cloned.1.call-done = bf16[8,512,256]{2,1,0:T(8,128)(2,1)} async-done(((bf16[1,512,256]{2,1,0:T(8,128)(2,1)}), bf16[8,512,256]{2,1,0:T(8,128)(2,1)}) %all-gather.11.cloned.1.call-update) | async-done | bytes 2097168 | tf_op jit(solution)/shard_map/all_gather | solution.py:662
  272.7 23.4 %shard_map.215 = (f32[144,1024]{1,0:T(8,128)S(1)}, f32[144,1024]{1,0:T(8,128)S(1)}, bf16[4,144,1024]{2,1,0:T(8,128)(2,1)S(1)}) custom-call(bf16[4,144,1024]{2,1,0:T(8,128)(2,1)S(1)} %bitcast.337, f32[144,1024]{1,0:T(8,128)S(1)} %get-tuple-element.54.x.value, f32[16,1024]{1,0:T(8,128)S(1)} %copy_bitcast_fusion.table), custom_call_target="tpu_custom_call" | custom-call | tf_op jit(solution)/shard_map/pallas_call | solution.py:175
  300.3 10.4 shard_map.217
  326.6 61.7 %all-gather.17.cloned.1.call-done = bf16[8,512,256]{2,1,0:T(8,128)(2,1)} async-done(((bf16[1,512,256]{2,1,0:T(8,128)(2,1)}), bf16[8,512,256]{2,1,0:T(8,128)(2,1)}) %all-gather.17.cloned.1.call-update) | async-done | bytes 2097168 | tf_op jit(solution)/shard_map/all_gather | solution.py:662
  393.2 23.5 %shard_map.218 = (f32[144,1024]{1,0:T(8,128)S(1)}, f32[144,1024]{1,0:T(8,128)S(1)}, bf16[4,144,1024]{2,1,0:T(8,128)(2,1)S(1)}) custom-call(bf16[4,144,1024]{2,1,0:T(8,128)(2,1)S(1)} %bitcast.327, f32[144,1024]{1,0:T(8,128)S(1)} %copy-done.8, f32[16,1024]{1,0:T(8,128)S(1)} %copy-done.1), custom_call_target="tpu_custom_call" | custom-call | tf_op jit(solution)/shard_map/pallas_call | solution.py:175
  419.7 23.4 %shard_map.219 = (f32[144,1024]{1,0:T(8,128)S(1)}, f32[8,1024]{1,0:T(8,128)S(1)}, bf16[4,144,1024]{2,1,0:T(8,128)(2,1)S(1)}) custom-call(bf16[4,144,1024]{2,1,0:T(8,128)(2,1)S(1)} %bitcast.336, f32[144,1024]{1,0:T(8,128)S(1)} %get-tuple-element.59.x.value, f32[144,1024]{1,0:T(8,128)S(1)} %copy-done.11, f32[16,1024]{1,0:T(8,128)S(1)} %copy-done.1), custom_call_target="tpu_custom_call" | custom-call | tf_op jit(solution)/shard_map/pallas_call | solution.py:175
  448.4 23.9 %shard_map.220 = (f32[144,1024]{1,0:T(8,128)S(1)}, f32[8,1024]{1,0:T(8,128)S(1)}, bf16[4,144,1024]{2,1,0:T(8,128)(2,1)S(1)}) custom-call(bf16[4,144,1024]{2,1,0:T(8,128)(2,1)S(1)} %bitcast.343, f32[144,1024]{1,0:T(8,128)S(1)} %get-tuple-element.59.x.value, f32[144,1024]{1,0:T(8,128)S(1)} %copy-done.11, f32[144,1024]{1,0:T(8,128)S(1)} %get-tuple-element.62.branch, ...), custom_call_target="tpu_custom_call" | custom-call | tf_op jit(solution)/shard_map/pallas_call | solution.py:175
  473.5 11.3 %shard_map.221 = (bf16[576,256]{1,0:T(8,128)(2,1)S(1)}, f32[576,512]{1,0:T(8,128)S(1)}, bf16[576,512]{1,0:T(8,128)(2,1)S(1)}) custom-call(bf16[576,768]{1,0:T(8,128)(2,1)S(1)} %add_convert_fusion.q.k.v, bf16[576,768]{1,0:T(8,128)(2,1)S(1)} %add_convert_fusion.q.k.v, bf16[576,768]{1,0:T(8,128)(2,1)S(1)} %add_convert_fusion.q.k.v, ...), custom_call_target="tpu_custom_call" | custom-call | tf_op jit(solution)/shard_map/pallas_call | solution.py:625
  497.2 26.9 %shard_map.223 = (f32[144,1024]{1,0:T(8,128)S(1)}, f32[8,1024]{1,0:T(8,128)S(1)}, bf16[4,144,1024]{2,1,0:T(8,128)(2,1)S(1)}) custom-call(bf16[4,144,1024]{2,1,0:T(8,128)(2,1)S(1)} %bitcast.342, f32[144,1024]{1,0:T(8,128)S(1)} %copy-done.9, f32[144,1024]{1,0:T(8,128)S(1)} %copy-done.31, f32[144,1024]{1,0:T(8,128)S(1)} %copy-done.29, f32[16,1024]{1,0:T(8,128)S(1)} %copy-done.2), custom_call_target="tpu_custom_call" | custom-call | tf_op jit(solution)/shard_map/pallas_call | solution.py:175
  531.8 23.9 %shard_map.224 = (f32[144,1024]{1,0:T(8,128)S(1)}, f32[8,1024]{1,0:T(8,128)S(1)}, bf16[4,144,1024]{2,1,0:T(8,128)(2,1)}) custom-call(bf16[4,144,1024]{2,1,0:T(8,128)(2,1)S(1)} %bitcast.344, f32[144,1024]{1,0:T(8,128)S(1)} %copy-done.6, f32[144,1024]{1,0:T(8,128)S(1)} %get-tuple-element.71.dx, f32[144,1024]{1,0:T(8,128)S(1)} %copy-done.27, ...), custom_call_target="tpu_custom_call" | custom-call | tf_op jit(solution)/shard_map/pallas_call | solution.py:175
  575.0 11.4 %shard_map.225 = (bf16[576,256]{1,0:T(8,128)(2,1)S(1)}, f32[576,512]{1,0:T(8,128)S(1)}, bf16[576,512]{1,0:T(8,128)(2,1)S(1)}) custom-call(bf16[576,768]{1,0:T(8,128)(2,1)S(1)} %add_convert_fusion.1.q.k.v, bf16[576,768]{1,0:T(8,128)(2,1)S(1)} %add_convert_fusion.1.q.k.v, bf16[576,768]{1,0:T(8,128)(2,1)S(1)} %add_convert_fusion.1.q.k.v, ...), custom_call_target="tpu_custom_call" | custom-call | tf_op jit(solution)/shard_map/pallas_call | solution.py:625
  637.3 24.1 %shard_map.227 = (bf16[2,8,144,128]{3,2,1,0:T(8,128)(2,1)S(1)}, f32[8,1024]{1,0:T(8,128)S(1)}) custom-call(bf16[4,144,1024]{2,1,0:T(8,128)(2,1)S(1)} %bitcast.345, f32[144,1024]{1,0:T(8,128)S(1)} %copy-done.4, f32[144,1024]{1,0:T(8,128)S(1)} %get-tuple-element.78.dx, f32[144,1024]{1,0:T(8,128)S(1)} %copy-done.25, f32[16,1024]{1,0:T(8,128)S(1)} %copy-done.2), custom_call_target="tpu_custom_call" | custom-call | tf_op jit(solution)/shard_map/pallas_call | solution.py:175
  663.3 31.0 %reduce-scatter.9.cloned.1.call-done = bf16[1,256,384]{1,2,0:T(8,128)(2,1)} async-done(((bf16[8,256,384]{1,2,0:T(8,128)(2,1)}), bf16[1,256,384]{1,2,0:T(8,128)(2,1)}) %reduce-scatter.9.cloned.1.call-update) | async-done | bytes 196624 | tf_op jit(solution)/shard_map/reduce_scatter | solution.py:676
  694.4 64.8 %reduce-scatter.21.cloned.1.call-done = bf16[1,512,256]{2,1,0:T(8,128)(2,1)} async-done(((bf16[8,512,256]{2,1,0:T(8,128)(2,1)}), bf16[1,512,256]{2,1,0:T(8,128)(2,1)}) %reduce-scatter.21.cloned.1.call-update) | async-done | bytes 262160 | tf_op jit(solution)/shard_map/reduce_scatter | solution.py:676
  759.2 61.1 %reduce-scatter.23.cloned.1.call-done = bf16[1,512,256]{2,1,0:T(8,128)(2,1)} async-done(((bf16[8,512,256]{2,1,0:T(8,128)(2,1)}), bf16[1,512,256]{2,1,0:T(8,128)(2,1)}) %reduce-scatter.23.cloned.1.call-update) | async-done | bytes 262160 | tf_op jit(solution)/shard_map/reduce_scatter | solution.py:676
  820.3 61.2 %reduce-scatter.17.cloned.1.call-done = bf16[1,256,512]{2,1,0:T(8,128)(2,1)} async-done(((bf16[8,256,512]{2,1,0:T(8,128)(2,1)}), bf16[1,256,512]{2,1,0:T(8,128)(2,1)}) %reduce-scatter.17.cloned.1.call-update) | async-done | bytes 262160 | tf_op jit(solution)/shard_map/reduce_scatter | solution.py:676
  881.5 61.3 %reduce-scatter.19.cloned.1.call-done = bf16[1,256,512]{2,1,0:T(8,128)(2,1)} async-done(((bf16[8,256,512]{2,1,0:T(8,128)(2,1)}), bf16[1,256,512]{2,1,0:T(8,128)(2,1)}) %reduce-scatter.19.cloned.1.call-update) | async-done | bytes 262160 | tf_op jit(solution)/shard_map/reduce_scatter | solution.py:676
  944.6 40.5 %all-reduce.5.cloned.1.call-done = f32[16,2,4,128]{3,0,2,1:T(8,128)} async-done(((f32[16,2,4,128]{3,0,2,1:T(8,128)}), f32[16,2,4,128]{3,0,2,1:T(8,128)}) %all-reduce.5.cloned.1.call-update) | async-done | bytes 65552 | tf_op jit(solution)/shard_map/psum | solution.py:804
  985.8 127.1 %psum.79 = f32[2,30,128]{2,1,0:T(8,128)S(1)} all-reduce(f32[2,30,128]{2,1,0:T(8,128)S(1)} %pad_maximum_fusion.4), channel_id=1, replica_groups=mesh['x'=4,'yl'=2,'co'=2,'yh'=2,'z'=4] {'x','yl','co','yh'}, use_global_device_ids=true, to_apply=%region_21.22 | all-reduce | flops 7680 | bytes 61440 | tf_op jit(solution)/shard_map/psum | solution.py:815
  (333 shorter events, 185.9 us)
Async XLA Ops:
  7.2 124.3 %all-gather.7.cloned.1.call-start = ((), (), s32[]{:S(2)}) async-start(), calls=%async_computation.8 | async-start | bytes 1769472 | tf_op jit(solution)/shard_map/all_gather | solution.py:662
  9.3 129.2 %all-gather.13.cloned.1.call-start = ((), (), s32[]{:S(2)}) async-start(), calls=%async_computation.11 | async-start | bytes 1769472 | tf_op jit(solution)/shard_map/all_gather | solution.py:662
  10.4 192.3 %all-gather.9.cloned.1.call-start = ((), (), s32[]{:S(2)}) async-start(), calls=%async_computation.9 | async-start | bytes 2359296 | tf_op jit(solution)/shard_map/all_gather | solution.py:662
  11.3 252.6 %all-gather.11.cloned.1.call-start = ((), (), s32[]{:S(2)}) async-start(), calls=%async_computation.10 | async-start | bytes 2359296 | tf_op jit(solution)/shard_map/all_gather | solution.py:662
  12.3 308.7 %all-gather.15.cloned.1.call-start = ((), (), s32[]{:S(2)}) async-start(), calls=%async_computation.12 | async-start | bytes 2359296 | tf_op jit(solution)/shard_map/all_gather | solution.py:662
  12.8 375.5 %all-gather.17.cloned.1.call-start = ((), (), s32[]{:S(2)}) async-start(), calls=%async_computation.13 | async-start | bytes 2359296 | tf_op jit(solution)/shard_map/all_gather | solution.py:662
  13.4 649.8 %reduce-scatter.15.cloned.1.call-start = ((), (), s32[]{:S(2)}) async-start(), calls=%async_computation.17 | async-start | bytes 589824 | tf_op jit(solution)/shard_map/reduce_scatter | solution.py:676
  59.0 30.2 %copy-start.66 = (bf16[1025,128]{1,0:T(8,128)(2,1)S(1)}, bf16[1025,128]{1,0:T(8,128)(2,1)}, u32[]{:S(2)}) copy-start(bf16[1025,128]{1,0:T(8,128)(2,1)} %param.12) | copy-start | bytes 787204
  59.9 29.4 %copy-start.77 = (f32[2,2,128]{2,1,0:T(2,128)S(1)}, f32[2,2,128]{2,1,0:T(2,128)}, u32[]{:S(2)}) copy-start(f32[2,2,128]{2,1,0:T(2,128)} %param.19) | copy-start | bytes 6148
  59.9 29.4 %copy-start.78 = (f32[2,2,128]{2,1,0:T(2,128)S(1)}, f32[2,2,128]{2,1,0:T(2,128)}, u32[]{:S(2)}) copy-start(f32[2,2,128]{2,1,0:T(2,128)} %param.21) | copy-start | bytes 6148
  59.9 29.4 %copy-start.79 = (f32[2,2,128]{2,1,0:T(2,128)S(1)}, f32[2,2,128]{2,1,0:T(2,128)}, u32[]{:S(2)}) copy-start(f32[2,2,128]{2,1,0:T(2,128)} %param.22) | copy-start | bytes 6148
  59.9 29.4 %copy-start.80 = (f32[2,2,128]{2,1,0:T(2,128)S(1)}, f32[2,2,128]{2,1,0:T(2,128)}, u32[]{:S(2)}) copy-start(f32[2,2,128]{2,1,0:T(2,128)} %param.20) | copy-start | bytes 6148
  131.4 141.2 %copy-start = (f32[16,1024]{1,0:T(8,128)}, f32[16,1024]{1,0:T(8,128)S(1)}, u32[]{:S(2)}) copy-start(f32[16,1024]{1,0:T(8,128)S(1)} %copy_bitcast_fusion.table) | copy-start | bytes 196612
  182.7 90.0 %copy-start.5 = (f32[144,1024]{1,0:T(8,128)}, f32[144,1024]{1,0:T(8,128)S(1)}, u32[]{:S(2)}) copy-start(f32[144,1024]{1,0:T(8,128)S(1)} %get-tuple-element.54.x.value) | copy-start | bytes 1769476
  494.7 168.5 %reduce-scatter.13.cloned.1.call-start = ((), (), s32[]{:S(2)}) async-start(), calls=%async_computation.16 | async-start | bytes 589824 | tf_op jit(solution)/shard_map/reduce_scatter | solution.py:676
  559.1 104.2 %reduce-scatter.11.cloned.1.call-start = ((), (), s32[]{:S(2)}) async-start(), calls=%async_computation.15 | async-start | bytes 1769472 | tf_op jit(solution)/shard_map/reduce_scatter | solution.py:676
  569.4 124.9 %reduce-scatter.9.cloned.1.call-start = ((), (), s32[]{:S(2)}) async-start(), calls=%async_computation.14 | async-start | bytes 1769472 | tf_op jit(solution)/shard_map/reduce_scatter | solution.py:676
  593.1 166.1 %reduce-scatter.21.cloned.1.call-start = ((), (), s32[]{:S(2)}) async-start(), calls=%async_computation.20 | async-start | bytes 2359296 | tf_op jit(solution)/shard_map/reduce_scatter | solution.py:676
  606.1 214.2 %reduce-scatter.23.cloned.1.call-start = ((), (), s32[]{:S(2)}) async-start(), calls=%async_computation.21 | async-start | bytes 2359296 | tf_op jit(solution)/shard_map/reduce_scatter | solution.py:676
  619.1 262.5 %reduce-scatter.17.cloned.1.call-start = ((), (), s32[]{:S(2)}) async-start(), calls=%async_computation.18 | async-start | bytes 2359296 | tf_op jit(solution)/shard_map/reduce_scatter | solution.py:676
  626.9 315.9 %reduce-scatter.19.cloned.1.call-start = ((), (), s32[]{:S(2)}) async-start(), calls=%async_computation.19 | async-start | bytes 2359296 | tf_op jit(solution)/shard_map/reduce_scatter | solution.py:676
  634.7 350.5 %all-reduce.5.cloned.1.call-start = ((), (), s32[]{:S(2)}) async-start(), calls=%async_computation.22 | async-start | bytes 131072 | tf_op jit(solution)/shard_map/psum | solution.py:804
  661.4 281.5 %copy-start.75 = (f32[1024]{0:T(1024)S(1)}, f32[1024]{0:T(1024)}, u32[]{:S(2)}) copy-start(f32[1024]{0:T(1024)} %get-tuple-element.122) | copy-start | bytes 12292
  663.2 451.6 %all-reduce.7.cloned.1.call-start = ((), (), s32[]{:S(2)}) async-start(), calls=%async_computation.23 | async-start | bytes 3145728 | tf_op jit(solution)/shard_map/psum | solution.py:677
  (73 other events, 422.7 us)
Sparse Core Ops, SparseCore 0:
  9.7 61.7 all-gather.6
  73.1 59.2 all-gather.12
  134.6 68.1 all-gather.8
  204.2 59.5 all-gather.10
  265.9 54.9 all-gather.14
  323.1 65.2 all-gather.16
  494.9 31.8 reduce-scatter.14
  559.2 31.6 reduce-scatter.12
  593.3 47.0 reduce-scatter.10
  642.6 51.6 reduce-scatter.8
  696.8 62.3 reduce-scatter.20
  761.4 58.8 reduce-scatter.22
  822.7 58.7 reduce-scatter.16
  883.8 58.9 reduce-scatter.18
  945.5 39.5 all-reduce.4
  988.0 51.7 all-reduce.6
